TPU v7x, 32 devices: a whole 2x2x4 slice. The times are simulated.
32 devices in a mesh: groups: 2 (over x), strip: 16 (over z, y, core).
Axes of the slice: x: 2, y: 2, z: 4, core: 2. Of those that a mesh axis runs over, the one named last changes fastest.
Arguments:
- queries: bfloat16 [32, 3, 128, 2240], P(('groups', 'strip')), parts along dimension 0, may hold values from -6 to 6
- keys: bfloat16 [32, 3, 128, 2240], P(('groups', 'strip')), parts along dimension 0, may hold values from -6 to 6
- values: bfloat16 [32, 3, 128, 2240], P(('groups', 'strip')), parts along dimension 0, may hold values from -6 to 6
- norm_gain: float32 [2240], replicated, may hold values from 0.1 to 1.9
- conv_weight: bfloat16 [3, 2240, 1152], P(None, None, 'strip'), may hold values from -0.078125 to 0.078125
Outputs:
- convolved: bfloat16 [32, 3, 128, 1152], P(('groups', 'strip')), parts along dimension 0
There are 2 independent parts, one for each index of `groups`. A program takes and returns all parts, laid end to end along the dimension named above; an argument that names none is the same for every part. Nothing has to cross between parts.
All inputs are finite; a program needn't handle non-finite values.
Results may differ from a plain program's by a relative error of at most 0.0051.
Values may be sent and summed in bfloat16 or wider, within the bound.
A program may use at most 128 MiB of HBM per device.

v0:
```python
import jax
import jax.numpy as jnp
from jax import lax
from jax.sharding import PartitionSpec as P

H = 20
DH = 112
TB = 4
FB = 3
P_SIZE = 128


def from_behind(block, axis, distance):
    devices = range(lax.axis_size(axis))
    route = [(i - distance, i) for i in devices if i - distance in devices]
    return lax.ppermute(block, axis, route)


def per_device(queries, keys, values, norm_gain, conv_weight):
    devices = lax.axis_size("strip")
    strips = devices // TB
    block_index = lax.axis_index("strip") // strips
    count = FB * P_SIZE
    width = H * DH
    key_heads = jax.nn.relu(keys).reshape(count, H, DH)
    value_heads = values.reshape(count, H, DH)
    key_value = jnp.einsum(
        "nhd,nhe->hde", key_heads, value_heads, preferred_element_type=jnp.float32
    )
    key_sums = jnp.sum(key_heads, axis=0, dtype=jnp.float32)
    state_len = H * DH * DH
    raw_len = state_len + width
    row_len = (raw_len + devices - 1) // devices * devices
    row = jnp.concatenate(
        [key_value.reshape(-1), key_sums.reshape(-1), jnp.zeros((row_len - raw_len,), jnp.float32)]
    )
    later_blocks = (jnp.arange(TB) >= block_index).astype(jnp.float32)[:, None]
    share = lax.psum_scatter(later_blocks * row[None, :], "strip", scatter_dimension=1, tiled=True)
    outgoing = jnp.broadcast_to(share[:, None, :], (TB, strips, share.shape[1])).reshape(
        devices, share.shape[1]
    )
    returned = lax.all_to_all(outgoing, "strip", split_axis=0, concat_axis=1, tiled=True).reshape(
        -1
    )
    state = returned[:state_len].reshape(H, DH, DH)
    summed = returned[state_len:raw_len].reshape(H, DH)
    state_rounded = state.astype(jnp.bfloat16)
    query_heads = jax.nn.relu(queries).reshape(count, H, DH)
    numer = jnp.einsum(
        "nhd,hde->nhe", query_heads, state_rounded, preferred_element_type=jnp.float32
    )
    denom = (
        jnp.einsum(
            "nhd,hd->nh", query_heads.astype(jnp.float32), summed, precision=lax.Precision.HIGHEST
        )
        + 1e-06
    )
    attended = (numer / denom[..., None]).reshape(count, width)
    scale = lax.rsqrt(jnp.mean(attended * attended, axis=-1, keepdims=True) + 1e-06)
    normed = (attended * scale * norm_gain).astype(jnp.bfloat16).reshape(FB, P_SIZE, width)
    rim = from_behind(normed[-2:], "strip", strips)
    extended = jnp.concatenate([rim, normed], axis=0)
    stacked = jnp.concatenate([normed, extended[1:-1], extended[:-2]], axis=-1).reshape(
        -1, 3 * width
    )
    full_taps = lax.all_gather(conv_weight, "strip", axis=2, tiled=True)
    mixed = jnp.dot(
        stacked, full_taps.reshape(3 * width, -1), preferred_element_type=jnp.float32
    ).astype(jnp.bfloat16)
    result = mixed.reshape(FB, P_SIZE, mixed.shape[-1])
    return result.reshape(1, FB, P_SIZE, result.shape[-1])


def solution(mesh):
    placed = (
        P(("groups", "strip"), None, None, None),
        P(("groups", "strip"), None, None, None),
        P(("groups", "strip"), None, None, None),
        P(),
        P(None, None, "strip"),
    )
    return jax.shard_map(
        per_device,
        mesh=mesh,
        in_specs=placed,
        out_specs=P(("groups", "strip"), None, None, None),
        check_vma=False,
    )
```

profile of v0, /device:TPU:24, one launch (start us, length us, event | category | flops | bytes accessed | tf_op | source)
XLA Modules:
  0.0 373.7 jit_solution(15843581912796238540)
XLA Ops:
  6.5 0.0 copy-start.4
  6.5 0.0 all-reduce.3.cloned.1.call-start
  6.5 2.0 convert_reduce_fusion
  8.5 0.0 copy-done.4
  8.6 1.3 broadcast_maximum_fusion.1
  9.9 8.8 %copy.43 = bf16[1,3,128,2240]{2,1,3,0:T(4,128)(2,1)S(1)} copy(bf16[1,3,128,2240]{2,3,1,0:T(8,128)(2,1)} %broadcast_maximum_fusion.1) | data formatting | bytes 3440640 | tf_op jit(solution)/shard_map/reshape | solution.py:25
  18.7 3.1 reshape.96
  21.8 8.8 %copy.44 = bf16[1,3,128,2240]{2,1,3,0:T(4,128)(2,1)S(1)} copy(bf16[1,3,128,2240]{2,3,1,0:T(8,128)(2,1)} %param.7) | data formatting | bytes 3440640 | tf_op jit(solution)/shard_map/reshape | solution.py:26
  30.6 3.1 reshape.97
  33.7 2.7 fusion.5
  36.4 0.9 reshape.88
  37.3 0.1 pad_maximum_fusion.1
  37.4 6.1 %broadcast_multiply_fusion = f32[4,253120]{1,0:T(4,128)} fusion(f32[253120]{0:T(1024)S(1)} %pad_maximum_fusion.1, f32[4]{0:T(128)S(1)} %compare_convert_fusion), kind=kLoop, calls=%fused_computation.8 | loop fusion | flops 1012480 | bytes 5062416 | tf_op jit(solution)/shard_map/mul | solution.py:38
  43.5 0.0 all-reduce.3.cloned.1.call-update
  43.5 0.0 all-gather.2.cloned.1.call-start
  43.5 0.7 all-gather.2.cloned.1.call-update
  44.3 0.0 copy-done.9
  44.3 0.6 dynamic-slice
  45.5 108.1 %all-reduce.3.cloned.1.call-done = f32[4,253120]{1,0:T(4,128)} async-done(((f32[4,253120]{1,0:T(4,128)}), f32[4,253120]{1,0:T(4,128)}) %all-reduce.3.cloned.1.call-update) | async-done | bytes 4049936
  153.6 1.1 constant_dynamic-slice_fusion
  154.7 0.2 broadcast_in_dim.2
  154.9 2.4 all_to_all.10
  157.3 0.0 copy-start.6
  157.3 5.8 %all-to-all-start = ((f32[16,1,15820]{2,1,0:T(1,128)}), f32[16,1,15820]{2,1,0:T(1,128)S(1)}, u32[]{:S(2)}, u32[]{:S(2)}) async-start(f32[16,1,15820]{2,1,0:T(1,128)} %all_to_all.10), calls=%async_computation | async-start | bytes 2031616 | tf_op jit(solution)/shard_map/all_to_all | solution.py:42
  163.1 0.0 copy-done.6
  163.1 0.1 broadcast_maximum_fusion
  163.2 12.2 %copy.45 = bf16[1,3,128,2240]{2,1,3,0:T(4,128)(2,1)S(1)} copy(bf16[1,3,128,2240]{2,3,1,0:T(8,128)(2,1)S(1)} %broadcast_maximum_fusion) | data formatting | bytes 3440640 | tf_op jit(solution)/shard_map/reshape | solution.py:48
  175.4 3.1 reshape.98
  178.5 23.6 %all-to-all-done = f32[16,1,15820]{2,1,0:T(1,128)S(1)} async-done(((f32[16,1,15820]{2,1,0:T(1,128)}), f32[16,1,15820]{2,1,0:T(1,128)S(1)}, u32[]{:S(2)}, u32[]{:S(2)}) %all-to-all-start) | async-done | bytes 1012512 | tf_op jit(solution)/shard_map/all_to_all | solution.py:42
  202.1 2.6 convert_reduce_fusion.1
  204.7 0.7 reshape.89
  205.4 1.5 convert_element_type.28
  206.9 0.0 copy-start.5
  206.9 3.7 reduce.3
  210.6 0.0 copy-start.7
  210.6 2.4 slice.23
  213.0 0.0 copy-done.5
  213.0 1.0 fusion.2
  214.0 0.0 copy-done.7
  214.0 3.0 multiply_reduce_fusion
  217.1 0.0 copy-start.8
  217.1 3.3 copy.35
  220.4 0.7 fusion.4
  221.1 0.0 copy-done.8
  221.1 0.4 multiply_convert_fusion.1
  221.4 0.0 copy-start.1
  221.4 1.2 copy-done.1
  222.7 0.0 copy-start
  222.7 1.1 slice.31
  223.8 2.7 copy.36
  226.5 1.5 collective-permute-start
  228.0 0.0 copy-done
  228.0 3.7 reshape.99
  231.7 4.5 %copy.47 = f32[3,128,2240]{2,1,0:T(8,128)S(1)} copy(f32[3,128,2240]{1,0,2:T(4,128)} %reshape.99) | data formatting | bytes 6881280 | tf_op jit(solution)/shard_map/reshape | solution.py:58
  236.2 1.6 multiply_convert_fusion
  237.8 0.0 copy-start.3
  237.8 77.4 %collective-permute-done = bf16[2,128,2240]{1,2,0:T(8,128)(2,1)} collective-permute-done((bf16[2,128,2240]{1,2,0:T(8,128)(2,1)}, bf16[2,128,2240]{1,2,0:T(8,128)(2,1)}, u32[]{:S(2)}, u32[]{:S(2)}) %collective-permute-start) | collective-permute-done | bytes 1146912 | tf_op jit(solution)/shard_map/ppermute | solution.py:16
  315.1 2.4 copy.38
  317.5 0.0 copy-done.3
  317.5 3.7 pad_maximum_fusion
  321.2 0.0 copy-done.2
  321.2 9.4 %concatenate.18 = bf16[384,6720]{1,0:T(8,128)(2,1)} concatenate(bf16[384,2240]{1,0:T(8,128)(2,1)S(1)} %copy-done.2, bf16[384,2240]{1,0:T(8,128)(2,1)} %bitcast.39, bf16[384,2240]{1,0:T(8,128)(2,1)} %bitcast.38), dimensions={1} | concatenate | bytes 10321920 | tf_op jit(solution)/shard_map/concatenate | solution.py:63
  330.6 22.1 %copy.39 = bf16[3,2240,1152]{2,1,0:T(8,128)(2,1)} copy(bf16[3,2240,1152]{1,2,0:T(8,128)(2,1)} %all-gather.2.cloned.1.call-done) | data formatting | bytes 30965760 | tf_op jit(solution)/shard_map/all_gather | solution.py:66
  352.7 14.1 %convolution_convert_fusion = bf16[384,1152]{1,0:T(8,128)(2,1)} fusion(bf16[384,6720]{1,0:T(8,128)(2,1)} %concatenate.18, bf16[6720,1152]{1,0:T(8,128)(2,1)} %bitcast.36), kind=kOutput, calls=%fused_computation.7 | convolution fusion | flops 5945868288 | bytes 21528576 | tf_op jit(solution)/shard_map/dot_general | solution.py:67
  (7 shorter events, 0.1 us)
Async XLA Ops:
  6.5 2.0 copy-start.4
  6.5 147.0 %all-reduce.3.cloned.1.call-start = ((), (), s32[]{:S(2)}) async-start(), calls=%async_computation.2 | async-start | bytes 8101888
  43.5 0.8 copy-start.9
  43.5 287.1 %all-gather.2.cloned.1.call-start = ((), (), s32[]{:S(2)}) async-start(), calls=%async_computation.1 | async-start | bytes 16920576 | tf_op jit(solution)/shard_map/all_gather | solution.py:66
  157.3 5.8 %copy-start.6 = (bf16[1,3,128,2240]{2,3,1,0:T(8,128)(2,1)S(1)}, bf16[1,3,128,2240]{2,3,1,0:T(8,128)(2,1)}, u32[]{:S(2)}) copy-start(bf16[1,3,128,2240]{2,3,1,0:T(8,128)(2,1)} %param.5) | copy-start | bytes 5160964
  157.3 44.8 %all-to-all-start = ((f32[16,1,15820]{2,1,0:T(1,128)}), f32[16,1,15820]{2,1,0:T(1,128)S(1)}, u32[]{:S(2)}, u32[]{:S(2)}) async-start(f32[16,1,15820]{2,1,0:T(1,128)} %all_to_all.10), calls=%async_computation | async-start | bytes 2031616 | tf_op jit(solution)/shard_map/all_to_all | solution.py:42
  206.9 6.1 %copy-start.5 = (bf16[384,20,112]{0,2,1:T(8,128)(2,1)S(1)}, bf16[384,20,112]{0,2,1:T(8,128)(2,1)}, u32[]{:S(2)}) copy-start(bf16[384,20,112]{0,2,1:T(8,128)(2,1)} %reshape.98) | copy-start | bytes 5160964
  210.6 3.5 copy-start.7
  217.1 4.0 %copy-start.8 = (f32[2240]{0:T(1024)S(1)}, f32[2240]{0:T(1024)}, u32[]{:S(2)}) copy-start(f32[2240]{0:T(1024)} %param.8) | copy-start | bytes 26884
  221.4 1.2 copy-start.1
  222.7 5.3 %copy-start = (f32[384,20,112]{0,2,1:T(8,128)S(1)}, f32[384,20,112]{0,2,1:T(8,128)}, u32[]{:S(2)}) copy-start(f32[384,20,112]{0,2,1:T(8,128)} %get-tuple-element.10) | copy-start | bytes 10321924
  226.5 88.6 %collective-permute-start = (bf16[2,128,2240]{1,2,0:T(8,128)(2,1)}, bf16[2,128,2240]{1,2,0:T(8,128)(2,1)}, u32[]{:S(2)}, u32[]{:S(2)}) collective-permute-start(bf16[2,128,2240]{1,2,0:T(8,128)(2,1)} %copy.36), channel_id=1, source_target_pairs={{0,4},{1,5},{2,6},{3,7},{4,8},{5,9},{6,10},{7,11},{8,12},{9,13},{1... | collective-permute-start | bytes 3440648 | tf_op jit(solution)/shard_map/ppermute | solution.py:16
  237.8 79.8 %copy-start.3 = (bf16[3,128,2240]{2,1,0:T(8,128)(2,1)S(1)}, bf16[3,128,2240]{2,1,0:T(8,128)(2,1)}, u32[]{:S(2)}) copy-start(bf16[3,128,2240]{2,1,0:T(8,128)(2,1)} %multiply_convert_fusion) | copy-start | bytes 5160964
  317.5 3.7 copy-start.2
Sparse Core Ops, SparseCore 0:
  43.6 109.8 all-reduce.2
  156.0 161.4 all-gather.1
where the time goes:
time: 375 us; the launch traced here: 374 us
  waiting for transfers between devices  210 us (56%)
  local copies, waits for them, and re-layouts  99.3 us (26%)
  other arithmetic  22.2 us (6%)
  matrix products  20.9 us (6%)
  between operations  14.2 us (4%)
  starting transfers between devices  7.32 us (2%)
    unnamed x3, waiting for transfers between devices  109 us
    ppermute x1, waiting for transfers between devices, from_behind(): return lax.ppermute(block, axis, route)  77.4 us
    all_to_all x1, waiting for transfers between devices, per_device(): lax.all_to_all(outgoing, 'strip', split_axis=0, concat_axis=1, tiled=True)  23.6 us
    all_gather x1, local copies, waits for them, and re-layouts, per_device(): full_taps = lax.all_gather(conv_weight, 'strip', axis=2, tiled=True)  22.1 us
    reshape x2, local copies, waits for them, and re-layouts, per_device(): query_heads = jax.nn.relu(queries).reshape(count, H, DH)  15.3 us
    dot_general x1, matrix products, per_device(): jnp.dot(stacked, full_taps.reshape(3 * width, -1), preferred_element_type...  14.1 us
    reshape x2, local copies, waits for them, and re-layouts, per_device(): key_heads = jax.nn.relu(keys).reshape(count, H, DH)  11.9 us
    reshape x2, local copies, waits for them, and re-layouts, per_device(): value_heads = values.reshape(count, H, DH)  11.9 us
  transfers between devices with their start and end apart: 4, of which 3 were waited for; matrix products, arithmetic and copies ran while one was open for 18% of the time, Pallas kernels for 0%

commit v1 on v0

v1 whole, which is shorter than its diff:
```python
import functools

import jax
import jax.numpy as jnp
from jax import lax
from jax.experimental import pallas as pl
from jax.experimental.pallas import tpu as pltpu
from jax.sharding import PartitionSpec as P

H = 20
TB = 4
MESH = pl.DeviceIdType.MESH


def kernel(n, q_ref, k_ref, v_ref, gain_ref, w_ref, o_ref, wbuf, own, sent, got, before,
           att, x, parts, wsend, wrecv, ssend, srecv, csend, crecv, rsend, rrecv):
    frames, pixels, width = q_ref.shape
    dh = width // H
    lanes = own.shape[2]
    tokens = frames * pixels
    back = x.shape[0] - frames
    rim = back * pixels
    cols = parts.shape[2]
    strips = n // TB
    me = lax.axis_index("strip")
    block = me // strips
    bits = [1 << b for b in range(n.bit_length() - 1)]

    def across(bit):
        return me + (1 - 2 * ((me // bit) % 2)) * bit

    def owner_of(m):
        dev = me
        for bit in bits:
            dev = dev + ((m // bit) % 2) * (1 - 2 * ((me // bit) % 2)) * bit
        return dev

    ahead = (me + strips) % n
    behind = (me + n - strips) % n
    barrier = pltpu.get_barrier_semaphore()
    for dev in [across(bit) for bit in bits] + [ahead, behind]:
        pl.semaphore_signal(barrier, inc=1, device_id={"strip": dev}, device_id_type=MESH)
    wbuf[0] = w_ref[...]
    pl.semaphore_wait(barrier, len(bits) + 2)

    def weight_copy(m, bit):
        return pltpu.make_async_remote_copy(
            src_ref=wbuf.at[m], dst_ref=wbuf.at[m + bit], send_sem=wsend.at[m + bit],
            recv_sem=wrecv.at[m + bit], device_id={"strip": across(bit)}, device_id_type=MESH)

    def landing(m):
        return pltpu.make_async_remote_copy(
            src_ref=wbuf.at[m], dst_ref=wbuf.at[m], send_sem=wsend.at[m],
            recv_sem=wrecv.at[m], device_id={"strip": across(1)}, device_id_type=MESH)

    rim_copy = pltpu.make_async_remote_copy(
        src_ref=q_ref.at[pl.ds(frames - back, back)], dst_ref=x.at[pl.ds(0, back)],
        send_sem=rsend, recv_sem=rrecv, device_id={"strip": ahead}, device_id_type=MESH)
    chain_copy = pltpu.make_async_remote_copy(
        src_ref=sent, dst_ref=before, send_sem=csend, recv_sem=crecv,
        device_id={"strip": ahead}, device_id_type=MESH)

    for bit in reversed(bits):
        weight_copy(0, bit).start()

    @pl.when(block < TB - 1)
    def _():
        rim_copy.start()

    ones = jnp.ones((tokens, lanes - dh), jnp.bfloat16)
    keys = k_ref[...].reshape(tokens, width)
    values = v_ref[...].reshape(tokens, width)
    for h in range(H):
        kh = jnp.maximum(keys[:, h * dh:(h + 1) * dh], 0)
        vh = jnp.concatenate([values[:, h * dh:(h + 1) * dh], ones], axis=1)
        own[h] = lax.dot_general(kh, vh, (((0,), (0,)), ((), ())),
                                 preferred_element_type=jnp.float32)

    for s in range(strips.bit_length() - 1):
        sent[...] = own[...].astype(jnp.bfloat16)
        copy = pltpu.make_async_remote_copy(
            src_ref=sent, dst_ref=got.at[s], send_sem=ssend.at[s], recv_sem=srecv.at[s],
            device_id={"strip": across(bits[s])}, device_id_type=MESH)
        copy.start()
        copy.wait()
        own[...] = own[...] + got[s].astype(jnp.float32)

    def early(z):
        m = z * strips
        landing(m).wait_recv()
        for bit in reversed(bits):
            if bit < (m & -m):
                weight_copy(m, bit).start()

    order = sorted(range(1, TB), key=lambda z: (bin(z).count("1"), -z))
    for z in order[:2]:
        early(z)

    @pl.when(block > 0)
    def _():
        chain_copy.wait_recv()
        sent[...] = (own[...] + before[...].astype(jnp.float32)).astype(jnp.bfloat16)

    @pl.when(block == 0)
    def _():
        sent[...] = own[...].astype(jnp.bfloat16)

    @pl.when(block < TB - 1)
    def _():
        chain_copy.start()

    for z in order[2:]:
        early(z)

    def attend(queries, state, first, count):
        rows = count * pixels
        total = jnp.zeros((rows, 1), jnp.float32)
        for h in range(H):
            qh = jnp.maximum(queries[:, h * dh:(h + 1) * dh], 0)
            both = jnp.dot(qh, state[h], preferred_element_type=jnp.float32)
            a = both[:, :dh] / (both[:, dh:dh + 1] + 1e-6)
            total = total + jnp.sum(a * a, axis=1, keepdims=True)
            att[pl.ds(0, rows), h * dh:(h + 1) * dh] = a
        scale = lax.rsqrt(total / width + 1e-6)
        x[pl.ds(first, count)] = (
            att[pl.ds(0, rows), :] * scale * gain_ref[...]
        ).astype(jnp.bfloat16).reshape(count, pixels, width)

    @pl.when(block > 0)
    def _():
        rim_copy.wait_recv()
        attend(x[pl.ds(0, back)].reshape(rim, width), before, 0, back)

    @pl.when(block == 0)
    def _():
        x[pl.ds(0, back)] = jnp.zeros((back, pixels, width), jnp.bfloat16)

    attend(q_ref[...].reshape(tokens, width), sent, back, frames)

    def mix(m):
        every = lax.dot_general(
            x[...].reshape(rim + tokens, width), wbuf[m], (((1,), (1,)), ((), ())),
            preferred_element_type=jnp.float32)
        total = every[rim:, :cols]
        for j in range(1, back + 1):
            first = rim - j * pixels
            total = total + every[first:first + tokens, j * cols:(j + 1) * cols]
        parts[owner_of(m)] = total.astype(jnp.bfloat16)

    def at_hand(z, carry):
        mix(z * strips)
        return carry

    def from_core(z, carry):
        m = z * strips + 1
        landing(m).wait_recv()
        mix(m)
        return carry

    def in_pairs(i, carry):
        m = (i % TB) * strips + 2 * (1 + i // TB)
        landing(m).wait_recv()
        for bit in reversed(bits):
            if 4 * bit <= strips:
                @pl.when(m % (2 * bit) == 0)
                def _():
                    weight_copy(m, bit).start()
        mix(m)
        landing(m + 1).wait_recv()
        mix(m + 1)
        return carry

    lax.fori_loop(0, TB, at_hand, 0)
    lax.fori_loop(0, TB, from_core, 0)
    lax.fori_loop(0, TB * (strips // 2 - 1), in_pairs, 0)
    for d in range(n):
        o_ref[:, d * cols:(d + 1) * cols] = parts[d]

    def leave(m, carry):
        landing(m).wait_send()
        return carry

    lax.fori_loop(1, n, leave, 0)

    @pl.when(block < TB - 1)
    def _():
        rim_copy.wait_send()
        chain_copy.wait_send()


def per_device(queries, keys, values, norm_gain, conv_weight):
    n = lax.axis_size("strip")
    _, frames, pixels, width = queries.shape
    taps, _, cols = conv_weight.shape
    dh = width // H
    lanes = (dh + 128) // 128 * 128
    stages = max((n // TB).bit_length() - 1, 1)
    tokens = frames * pixels
    bf16, f32 = jnp.bfloat16, jnp.float32
    dma = pltpu.SemaphoreType.DMA
    out = pl.pallas_call(
        functools.partial(kernel, n),
        out_shape=jax.ShapeDtypeStruct((tokens, n * cols), bf16),
        in_specs=[pl.BlockSpec(memory_space=pltpu.VMEM)] * 5,
        out_specs=pl.BlockSpec(memory_space=pltpu.VMEM),
        scratch_shapes=[
            pltpu.VMEM((n, taps * cols, width), bf16),
            pltpu.VMEM((H, dh, lanes), f32),
            pltpu.VMEM((H, dh, lanes), bf16),
            pltpu.VMEM((stages, H, dh, lanes), bf16),
            pltpu.VMEM((H, dh, lanes), bf16),
            pltpu.VMEM((tokens, width), f32),
            pltpu.VMEM((frames + taps - 1, pixels, width), bf16),
            pltpu.VMEM((n, tokens, cols), bf16),
            dma((n,)), dma((n,)), dma((stages,)), dma((stages,)),
            dma, dma, dma, dma,
        ],
        compiler_params=pltpu.CompilerParams(
            collective_id=0, has_side_effects=True, vmem_limit_bytes=62 * 1024 * 1024),
    )(queries[0], keys[0], values[0], norm_gain[None, :], conv_weight.transpose(0, 2, 1).reshape(taps * cols, width))
    return out.reshape(1, frames, pixels, n * cols)


def solution(mesh):
    placed = (
        P(("groups", "strip"), None, None, None),
        P(("groups", "strip"), None, None, None),
        P(("groups", "strip"), None, None, None),
        P(),
        P(None, None, "strip"),
    )
    return jax.shard_map(
        per_device,
        mesh=mesh,
        in_specs=placed,
        out_specs=P(("groups", "strip"), None, None, None),
        check_vma=False,
    )
```

time: 375 us -> 190 us (0.51)
  waiting for transfers between devices: 210 us -> 0 us
  Pallas kernels: 0 us -> 178 us
  local copies, waits for them, and re-layouts: 99.3 us -> 11.9 us
  other arithmetic: 22.2 us -> 0 us
  matrix products: 20.9 us -> 0 us
  between operations: 14.2 us -> 0.01 us
  starting transfers between devices: 7.32 us -> 0 us
    pallas_call x0 -> x1, Pallas kernels: none -> 178 us  [per_device(): pl.pallas_call(functools.partial(kernel, n), out_shape=jax.ShapeDtypeStru...]
    unnamed x3 -> x0, waiting for transfers between devices: 109 us -> none
    ppermute x1 -> x0, waiting for transfers between devices: 77.4 us -> none  [from_behind(): return lax.ppermute(block, axis, route)]
    reshape x11 -> x0, local copies, waits for them, and re-layouts: 52.1 us -> none  [the longest x2 15.3 us: per_device(): query_heads = jax.nn.relu(queries).reshape(count, H, DH)]
    all_to_all x1 -> x0, waiting for transfers between devices: 23.6 us -> none  [per_device(): lax.all_to_all(outgoing, 'strip', split_axis=0, concat_axis=1, tiled=True)]
    all_gather x1 -> x0, local copies, waits for them, and re-layouts: 22.1 us -> none  [per_device(): full_taps = lax.all_gather(conv_weight, 'strip', axis=2, tiled=True)]
    dot_general x4 -> x0, matrix products: 20.9 us -> none  [the longest x1 14.1 us: per_device(): jnp.dot(stacked, full_taps.reshape(3 * width, -1), preferred_element_type...]
    concatenate x1 -> x0, local copies, waits for them, and re-layouts: 9.4 us -> none  [per_device(): jnp.concatenate([normed, extended[1:-1], extended[:-2]], axis=-1)]
  transfers between devices with their start and end apart: 4 -> 0, of which waited for: 3 -> 0; matrix products, arithmetic and copies ran while one was open for 18% -> 0% of each run, Pallas kernels for 0% -> 0%
where the time goes in v1:
time: 190 us
  Pallas kernels  178 us (94%)
  local copies, waits for them, and re-layouts  11.9 us (6%)
    pallas_call x1, Pallas kernels, per_device(): pl.pallas_call(functools.partial(kernel, n), out_shape=jax.ShapeDtypeStru...  178 us
    unnamed x8, local copies, waits for them, and re-layouts  10.5 us

profile of v1, /device:TPU:24, one launch (start us, length us, event | category | flops | bytes accessed | tf_op | source)
XLA Modules:
  0.0 189.9 jit_solution(17955670845184092300)
XLA Ops:
  0.0 0.0 copy-start
  0.0 1.4 broadcast_in_dim.3.gain_ref
  1.4 3.9 %copy.6 = bf16[1,3,128,2240]{3,2,1,0:T(8,128)(2,1)} copy(bf16[1,3,128,2240]{2,3,1,0:T(8,128)(2,1)} %param.5) | data formatting | bytes 3440640 | tf_op args[0]
  5.3 0.0 copy-start.1
  5.3 0.0 copy-done
  5.3 2.2 %copy.7 = bf16[1,3,128,2240]{3,2,1,0:T(8,128)(2,1)} copy(bf16[1,3,128,2240]{2,3,1,0:T(8,128)(2,1)S(1)} %copy-done) | data formatting | bytes 3440640 | tf_op args[1]
  7.5 0.0 copy-done.1
  7.5 2.2 %copy.8 = bf16[1,3,128,2240]{3,2,1,0:T(8,128)(2,1)} copy(bf16[1,3,128,2240]{2,3,1,0:T(8,128)(2,1)S(1)} %copy-done.1) | data formatting | bytes 3440640 | tf_op args[2]
  9.8 178.0 %shard_map.55 = bf16[384,1152]{1,0:T(8,128)(2,1)} custom-call(bf16[3,128,2240]{2,1,0:T(8,128)(2,1)} %bitcast.7, bf16[3,128,2240]{2,1,0:T(8,128)(2,1)} %bitcast.8, bf16[3,128,2240]{2,1,0:T(8,128)(2,1)} %bitcast.9, f32[1,2240]{1,0:T(1,128)} %broadcast_in_dim.3.gain_ref, bf16[216,2240]{1,0:T(8,128)(2,1)} %bitcast.11), custom_call_target="tpu_custom_call" | custom-call | tf_op jit(solution)/shard_map/pallas_call | solution.py:201
  187.8 2.1 %copy.10 = bf16[1,3,128,1152]{3,2,1,0:T(8,128)(2,1)} copy(bf16[1,3,128,1152]{3,2,1,0:T(8,128)(2,1)} %bitcast.10) | data formatting | bytes 1769472
Async XLA Ops:
  0.0 5.3 %copy-start = (bf16[1,3,128,2240]{2,3,1,0:T(8,128)(2,1)S(1)}, bf16[1,3,128,2240]{2,3,1,0:T(8,128)(2,1)}, u32[]{:S(2)}) copy-start(bf16[1,3,128,2240]{2,3,1,0:T(8,128)(2,1)} %param.6) | copy-start | bytes 5160964
  5.3 2.2 %copy-start.1 = (bf16[1,3,128,2240]{2,3,1,0:T(8,128)(2,1)S(1)}, bf16[1,3,128,2240]{2,3,1,0:T(8,128)(2,1)}, u32[]{:S(2)}) copy-start(bf16[1,3,128,2240]{2,3,1,0:T(8,128)(2,1)} %param.7) | copy-start | bytes 5160964

commit v2 on v1

--- a/solution.py
+++ b/solution.py
@@ -13,7 +13,8 @@
 
 
 def kernel(n, q_ref, k_ref, v_ref, gain_ref, w_ref, o_ref, wbuf, own, sent, got, before,
-           att, x, parts, wsend, wrecv, ssend, srecv, csend, crecv, rsend, rrecv):
+           att, x, parts, wsend, wrecv, ssend, srecv, csend, crecv, rsend, rrecv,
+           xsend):
     frames, pixels, width = q_ref.shape
     dh = width // H
     lanes = own.shape[2]
@@ -35,18 +36,34 @@
             dev = dev + ((m // bit) % 2) * (1 - 2 * ((me // bit) % 2)) * bit
         return dev
 
+    group = lax.axis_index("groups")
     ahead = (me + strips) % n
     behind = (me + n - strips) % n
     barrier = pltpu.get_barrier_semaphore()
     for dev in [across(bit) for bit in bits] + [ahead, behind]:
         pl.semaphore_signal(barrier, inc=1, device_id={"strip": dev}, device_id_type=MESH)
+    pl.semaphore_signal(barrier, inc=1, device_id={"groups": 1 - group}, device_id_type=MESH)
     wbuf[0] = w_ref[...]
-    pl.semaphore_wait(barrier, len(bits) + 2)
+    pl.semaphore_wait(barrier, len(bits) + 3)
 
     def weight_copy(m, bit):
         return pltpu.make_async_remote_copy(
             src_ref=wbuf.at[m], dst_ref=wbuf.at[m + bit], send_sem=wsend.at[m + bit],
             recv_sem=wrecv.at[m + bit], device_id={"strip": across(bit)}, device_id_type=MESH)
+
+    def twin_copy(m):
+        return pltpu.make_async_remote_copy(
+            src_ref=wbuf.at[m], dst_ref=wbuf.at[m], send_sem=xsend.at[m],
+            recv_sem=wrecv.at[m], device_id={"groups": 1 - group}, device_id_type=MESH)
+
+    def forward(m, limit, side):
+        for bit in reversed(bits):
+            if bit < limit and bit in (strips, strips // 2):
+                @pl.when(group == side)
+                def _():
+                    weight_copy(m, bit).start()
+            elif bit < limit:
+                weight_copy(m, bit).start()
 
     def landing(m):
         return pltpu.make_async_remote_copy(
@@ -60,8 +77,7 @@
         src_ref=sent, dst_ref=before, send_sem=csend, recv_sem=crecv,
         device_id={"strip": ahead}, device_id_type=MESH)
 
-    for bit in reversed(bits):
-        weight_copy(0, bit).start()
+    forward(0, n, 0)
 
     @pl.when(block < TB - 1)
     def _():
@@ -85,16 +101,14 @@
         copy.wait()
         own[...] = own[...] + got[s].astype(jnp.float32)
 
-    def early(z):
-        m = z * strips
-        landing(m).wait_recv()
-        for bit in reversed(bits):
-            if bit < (m & -m):
-                weight_copy(m, bit).start()
-
-    order = sorted(range(1, TB), key=lambda z: (bin(z).count("1"), -z))
-    for z in order[:2]:
-        early(z)
+    far = 2 * strips
+    landing(far).wait_recv()
+    forward(far, far, 1)
+    mine = strips + far * group
+    theirs = strips + far * (1 - group)
+    landing(mine).wait_recv()
+    forward(mine, strips, group)
+    twin_copy(mine).start()
 
     @pl.when(block > 0)
     def _():
@@ -109,8 +123,8 @@
     def _():
         chain_copy.start()
 
-    for z in order[2:]:
-        early(z)
+    landing(theirs).wait_recv()
+    forward(theirs, strips // 2, group)
 
     def attend(queries, state, first, count):
         rows = count * pixels
@@ -158,8 +172,13 @@
         return carry
 
     def in_pairs(i, carry):
-        m = (i % TB) * strips + 2 * (1 + i // TB)
+        m = ((i + group * (TB // 2)) % TB) * strips + 2 * (1 + i // TB)
         landing(m).wait_recv()
+
+        @pl.when((m % strips == strips // 2) & ((m // far) % 2 == group))
+        def _():
+            twin_copy(m).start()
+
         for bit in reversed(bits):
             if 4 * bit <= strips:
                 @pl.when(m % (2 * bit) == 0)
@@ -177,7 +196,17 @@
         o_ref[:, d * cols:(d + 1) * cols] = parts[d]
 
     def leave(m, carry):
-        landing(m).wait_send()
+        shared = (m % far == strips) | (m % strips == strips // 2)
+        fetched = (m // far) % 2 == group
+
+        @pl.when(jnp.logical_not(shared) | fetched)
+        def _():
+            landing(m).wait_send()
+
+        @pl.when(shared & fetched)
+        def _():
+            twin_copy(m).wait_send()
+
         return carry
 
     lax.fori_loop(1, n, leave, 0)
@@ -213,7 +242,7 @@
             pltpu.VMEM((frames + taps - 1, pixels, width), bf16),
             pltpu.VMEM((n, tokens, cols), bf16),
             dma((n,)), dma((n,)), dma((stages,)), dma((stages,)),
-            dma, dma, dma, dma,
+            dma, dma, dma, dma, dma((n,)),
         ],
         compiler_params=pltpu.CompilerParams(
             collective_id=0, has_side_effects=True, vmem_limit_bytes=62 * 1024 * 1024),

time: 190 us -> 200 us (1.053)
  Pallas kernels: 178 us -> 187 us
    pallas_call x1, Pallas kernels: 178 us -> 187 us  [per_device(): pl.pallas_call(functools.partial(kernel, n), out_shape=jax.ShapeDtypeStru...]
where the time goes in v2:
time: 200 us; the launch traced here: 199 us
  Pallas kernels  187 us (94%)
  local copies, waits for them, and re-layouts  11.9 us (6%)
    pallas_call x1, Pallas kernels, per_device(): pl.pallas_call(functools.partial(kernel, n), out_shape=jax.ShapeDtypeStru...  187 us
    unnamed x8, local copies, waits for them, and re-layouts  10.5 us

profile of v2, /device:TPU:24, one launch (start us, length us, event | category | flops | bytes accessed | tf_op | source)
XLA Modules:
  0.0 198.8 jit_solution(4338751860142443532)
XLA Ops:
  0.0 0.0 copy-start
  0.0 1.4 broadcast_in_dim.3.gain_ref
  1.4 3.9 %copy.6 = bf16[1,3,128,2240]{3,2,1,0:T(8,128)(2,1)} copy(bf16[1,3,128,2240]{2,3,1,0:T(8,128)(2,1)} %param.5) | data formatting | bytes 3440640 | tf_op args[0]
  5.3 0.0 copy-start.1
  5.3 0.0 copy-done
  5.3 2.2 %copy.7 = bf16[1,3,128,2240]{3,2,1,0:T(8,128)(2,1)} copy(bf16[1,3,128,2240]{2,3,1,0:T(8,128)(2,1)S(1)} %copy-done) | data formatting | bytes 3440640 | tf_op args[1]
  7.5 0.0 copy-done.1
  7.5 2.2 %copy.8 = bf16[1,3,128,2240]{3,2,1,0:T(8,128)(2,1)} copy(bf16[1,3,128,2240]{2,3,1,0:T(8,128)(2,1)S(1)} %copy-done.1) | data formatting | bytes 3440640 | tf_op args[2]
  9.8 186.9 %shard_map.55 = bf16[384,1152]{1,0:T(8,128)(2,1)} custom-call(bf16[3,128,2240]{2,1,0:T(8,128)(2,1)} %bitcast.7, bf16[3,128,2240]{2,1,0:T(8,128)(2,1)} %bitcast.8, bf16[3,128,2240]{2,1,0:T(8,128)(2,1)} %bitcast.9, f32[1,2240]{1,0:T(1,128)} %broadcast_in_dim.3.gain_ref, bf16[216,2240]{1,0:T(8,128)(2,1)} %bitcast.11), custom_call_target="tpu_custom_call" | custom-call | tf_op jit(solution)/shard_map/pallas_call | solution.py:230
  196.6 2.1 %copy.10 = bf16[1,3,128,1152]{3,2,1,0:T(8,128)(2,1)} copy(bf16[1,3,128,1152]{3,2,1,0:T(8,128)(2,1)} %bitcast.10) | data formatting | bytes 1769472
Async XLA Ops:
  0.0 5.3 %copy-start = (bf16[1,3,128,2240]{2,3,1,0:T(8,128)(2,1)S(1)}, bf16[1,3,128,2240]{2,3,1,0:T(8,128)(2,1)}, u32[]{:S(2)}) copy-start(bf16[1,3,128,2240]{2,3,1,0:T(8,128)(2,1)} %param.6) | copy-start | bytes 5160964
  5.3 2.2 %copy-start.1 = (bf16[1,3,128,2240]{2,3,1,0:T(8,128)(2,1)S(1)}, bf16[1,3,128,2240]{2,3,1,0:T(8,128)(2,1)}, u32[]{:S(2)}) copy-start(bf16[1,3,128,2240]{2,3,1,0:T(8,128)(2,1)} %param.7) | copy-start | bytes 5160964

commit v3 on v1

--- a/solution.py
+++ b/solution.py
@@ -13,7 +13,8 @@
 
 
 def kernel(n, q_ref, k_ref, v_ref, gain_ref, w_ref, o_ref, wbuf, own, sent, got, before,
-           att, x, parts, wsend, wrecv, ssend, srecv, csend, crecv, rsend, rrecv):
+           att, x, parts, wsend, wrecv, ssend, srecv, csend, crecv, rsend, rrecv,
+           xsend):
     frames, pixels, width = q_ref.shape
     dh = width // H
     lanes = own.shape[2]
@@ -35,18 +36,43 @@
             dev = dev + ((m // bit) % 2) * (1 - 2 * ((me // bit) % 2)) * bit
         return dev
 
+    group = lax.axis_index("groups")
     ahead = (me + strips) % n
     behind = (me + n - strips) % n
     barrier = pltpu.get_barrier_semaphore()
     for dev in [across(bit) for bit in bits] + [ahead, behind]:
         pl.semaphore_signal(barrier, inc=1, device_id={"strip": dev}, device_id_type=MESH)
+    pl.semaphore_signal(barrier, inc=1, device_id={"groups": 1 - group}, device_id_type=MESH)
     wbuf[0] = w_ref[...]
-    pl.semaphore_wait(barrier, len(bits) + 2)
+    pl.semaphore_wait(barrier, len(bits) + 3)
 
     def weight_copy(m, bit):
         return pltpu.make_async_remote_copy(
             src_ref=wbuf.at[m], dst_ref=wbuf.at[m + bit], send_sem=wsend.at[m + bit],
             recv_sem=wrecv.at[m + bit], device_id={"strip": across(bit)}, device_id_type=MESH)
+
+    def twin_copy(m):
+        return pltpu.make_async_remote_copy(
+            src_ref=wbuf.at[m], dst_ref=wbuf.at[m], send_sem=xsend.at[m],
+            recv_sem=wrecv.at[m], device_id={"groups": 1 - group}, device_id_type=MESH)
+
+    def ours(m):
+        return (m // strips) % 2 == group
+
+    def send(m, bit):
+        if bit > 1:
+            weight_copy(m, bit).start()
+        else:
+            @pl.when(ours(m))
+            def _():
+                weight_copy(m, bit).start()
+
+    def odd(m):
+        landing(m).wait_recv()
+
+        @pl.when(ours(m))
+        def _():
+            twin_copy(m).start()
 
     def landing(m):
         return pltpu.make_async_remote_copy(
@@ -61,7 +87,7 @@
         device_id={"strip": ahead}, device_id_type=MESH)
 
     for bit in reversed(bits):
-        weight_copy(0, bit).start()
+        send(0, bit)
 
     @pl.when(block < TB - 1)
     def _():
@@ -90,7 +116,7 @@
         landing(m).wait_recv()
         for bit in reversed(bits):
             if bit < (m & -m):
-                weight_copy(m, bit).start()
+                send(m, bit)
 
     order = sorted(range(1, TB), key=lambda z: (bin(z).count("1"), -z))
     for z in order[:2]:
@@ -153,7 +179,7 @@
 
     def from_core(z, carry):
         m = z * strips + 1
-        landing(m).wait_recv()
+        odd(m)
         mix(m)
         return carry
 
@@ -164,9 +190,9 @@
             if 4 * bit <= strips:
                 @pl.when(m % (2 * bit) == 0)
                 def _():
-                    weight_copy(m, bit).start()
+                    send(m, bit)
         mix(m)
-        landing(m + 1).wait_recv()
+        odd(m + 1)
         mix(m + 1)
         return carry
 
@@ -177,7 +203,14 @@
         o_ref[:, d * cols:(d + 1) * cols] = parts[d]
 
     def leave(m, carry):
-        landing(m).wait_send()
+        @pl.when((m % 2 == 0) | ours(m))
+        def _():
+            landing(m).wait_send()
+
+        @pl.when((m % 2 == 1) & ours(m))
+        def _():
+            twin_copy(m).wait_send()
+
         return carry
 
     lax.fori_loop(1, n, leave, 0)
@@ -213,7 +246,7 @@
             pltpu.VMEM((frames + taps - 1, pixels, width), bf16),
             pltpu.VMEM((n, tokens, cols), bf16),
             dma((n,)), dma((n,)), dma((stages,)), dma((stages,)),
-            dma, dma, dma, dma,
+            dma, dma, dma, dma, dma((n,)),
         ],
         compiler_params=pltpu.CompilerParams(
             collective_id=0, has_side_effects=True, vmem_limit_bytes=62 * 1024 * 1024),

time: 190 us -> 364 us (1.92)
  Pallas kernels: 178 us -> 352 us
    pallas_call x1, Pallas kernels: 178 us -> 352 us  [per_device(): pl.pallas_call(functools.partial(kernel, n), out_shape=jax.ShapeDtypeStru...]
where the time goes in v3:
time: 364 us
  Pallas kernels  352 us (97%)
  local copies, waits for them, and re-layouts  11.9 us (3%)
    pallas_call x1, Pallas kernels, per_device(): pl.pallas_call(functools.partial(kernel, n), out_shape=jax.ShapeDtypeStru...  352 us
    unnamed x8, local copies, waits for them, and re-layouts  10.5 us

profile of v3, /device:TPU:24, one launch (start us, length us, event | category | flops | bytes accessed | tf_op | source)
XLA Modules:
  0.0 363.7 jit_solution(17067000203520685967)
XLA Ops:
  0.0 0.0 copy-start
  0.0 1.4 broadcast_in_dim.3.gain_ref
  1.4 3.9 %copy.6 = bf16[1,3,128,2240]{3,2,1,0:T(8,128)(2,1)} copy(bf16[1,3,128,2240]{2,3,1,0:T(8,128)(2,1)} %param.5) | data formatting | bytes 3440640 | tf_op args[0]
  5.3 0.0 copy-start.1
  5.3 0.0 copy-done
  5.3 2.2 copy.7
  7.5 0.0 copy-done.1
  7.5 2.2 copy.8
  9.8 351.7 %shard_map.55 = bf16[384,1152]{1,0:T(8,128)(2,1)} custom-call(bf16[3,128,2240]{2,1,0:T(8,128)(2,1)} %bitcast.7, bf16[3,128,2240]{2,1,0:T(8,128)(2,1)} %bitcast.8, bf16[3,128,2240]{2,1,0:T(8,128)(2,1)} %bitcast.9, f32[1,2240]{1,0:T(1,128)} %broadcast_in_dim.3.gain_ref, bf16[216,2240]{1,0:T(8,128)(2,1)} %bitcast.11), custom_call_target="tpu_custom_call" | custom-call | tf_op jit(solution)/shard_map/pallas_call | solution.py:234
  361.5 2.1 copy.10
Async XLA Ops:
  0.0 5.3 %copy-start = (bf16[1,3,128,2240]{2,3,1,0:T(8,128)(2,1)S(1)}, bf16[1,3,128,2240]{2,3,1,0:T(8,128)(2,1)}, u32[]{:S(2)}) copy-start(bf16[1,3,128,2240]{2,3,1,0:T(8,128)(2,1)} %param.6) | copy-start | bytes 5160964
  5.3 2.2 copy-start.1
